TPU v7x, 128 devices: a whole 4x4x4 slice. The times are simulated.
128 devices in a mesh: row: 8 (over y_lo, z), col: 16 (over x, y_hi, core).
Axes of the slice: x: 4, y: 4 (y_hi: 2, y_lo: 2; y = y_hi * 2 + y_lo), z: 4, core: 2. Of those that a mesh axis runs over, the one named last changes fastest.
Arguments:
- x_blocks: bfloat16 [2048, 2048, 128], P('row', 'col'), may hold values from -0.046875 to 0.046875
- block_ids: int32 [2048, 16], P('row', 'col'), may hold values from 0 to 511, as said below
- margins: float32 [32768], P('row'), may hold values from -6 to 6
- deleted: int32 [4096], P('row'), may hold values from 0 to 32767, as said below
- grads: float32 [32768, 128], P('col'), may hold values from -6 to 6
Outputs:
- solution: float32 [32768, 128], P('col')
- residual: float32 [32768, 128], P('col')
Inputs may be any that keep to these rules, and one draw needn't show every extreme that they name: `block_ids`: each device's 256 entries are distinct and rise; each device lists the first and the last block of its grid. `deleted`: the 512 entries of row shard r are distinct rows of that shard, r * 4096 and up; each shard deletes its first and its last row.
All inputs are finite; a program needn't handle non-finite values.
Results may differ from a plain program's by a relative error of at most 0.015.
Values may be sent and summed in bfloat16 or wider, within the bound.
A program may use at most 128 MiB of HBM per device.

v0:
```python
import jax
import jax.numpy as jnp
from jax import lax
from jax.sharding import Mesh
from jax.sharding import PartitionSpec as P

ITERS = 3
ROW = ("row_0", "row_1")
COL = ("col_0", "col_1", "col_2")
ROW_COL = ("row_0", "row_1", "col_0", "col_1", "col_2")
highest = lax.Precision.HIGHEST
ridge_weight = 0.2


def cut_along(shard, dim, size):
    before, after = (shard.shape[:dim], shard.shape[dim + 1 :])
    return jnp.moveaxis(shard.reshape(*before, size, -1, *after), dim, 0)


def sent_and_summed(shard, axis, dim):
    pieces = cut_along(shard, dim, lax.axis_size(axis))
    arrived = lax.all_to_all(pieces, axis, split_axis=0, concat_axis=0, tiled=True)
    return arrived.sum(axis=0)


def from_everyone(shard, axis):
    size = lax.axis_size(axis)
    return lax.all_to_all(
        jnp.broadcast_to(shard[None], (size, *shard.shape)), axis, 0, 0, tiled=True
    )


def laid_out(pieces, dim):
    shape = list(pieces.shape[1:])
    shape[dim] *= pieces.shape[0]
    return jnp.moveaxis(pieces, 0, dim).reshape(shape)


def gather_directly(shard, axis, dim):
    pieces = from_everyone(shard, axis)
    return laid_out(pieces, dim)


def by_axis(shard, axes):
    for axis in axes:
        shard = lax.psum(shard, axis)
    return shard


def in_one_piece(arrays, axis, dim, along):
    both = jnp.concatenate(arrays, axis=along)
    result, at, outs = (lax.all_gather(both, axis, axis=dim, tiled=True), 0, [])
    for a in arrays:
        outs.append(lax.slice_in_dim(result, at, at + a.shape[along], axis=along))
        at += a.shape[along]
    return tuple(outs)


def on_device(x_blocks, block_ids, margins, deleted, grads):
    block_width = x_blocks.shape[1]
    feature_rows = grads.shape[0]
    directions = grads.shape[1]
    row_count = margins.shape[0]
    row_blocks = row_count // block_width
    feature_blocks = feature_rows // block_width
    pattern = block_ids[:, 0]
    block_row = pattern // feature_blocks
    block_column = pattern % feature_blocks
    row_select = (block_row[:, None] == jnp.arange(row_blocks, dtype=jnp.int32)[None, :]).astype(
        jnp.float32
    )
    column_select = (
        block_column[:, None] == jnp.arange(feature_blocks, dtype=jnp.int32)[None, :]
    ).astype(jnp.float32)
    global_rows = lax.axis_index(ROW) * row_count + jnp.arange(row_count, dtype=jnp.int32)
    removed = jnp.any(global_rows[:, None] == deleted[None, :], axis=1)
    logistic = jax.nn.sigmoid(margins)
    weights_flat = jnp.where(removed, 0.0, logistic * (1.0 - logistic))
    row_share_count = row_count // lax.axis_size(COL)
    row_offset = lax.axis_index(COL) * row_share_count
    share_rows = feature_rows // lax.axis_size(ROW)
    offset = lax.axis_index(ROW) * share_rows
    residual = lax.dynamic_slice_in_dim(grads, offset, share_rows, 0)
    solution = jnp.zeros_like(residual)
    direction = residual
    mine = residual
    norm_now = by_axis(jnp.sum(mine * mine, axis=0), ROW_COL)
    for iteration in range(ITERS):
        apply_rounded = direction.astype(jnp.bfloat16)
        gathered = gather_directly(apply_rounded, ROW, 0)
        picked_tiles = gathered.reshape(feature_blocks, block_width, directions)[block_column]
        forward = jnp.einsum(
            "bij,bjk->bik", x_blocks, picked_tiles, preferred_element_type=jnp.float32
        )
        partial_rows = jnp.einsum("br,bik->rik", row_select, forward, precision=highest)
        flat_rows = partial_rows.reshape(row_count, directions)
        own_sum = sent_and_summed(flat_rows, COL, 0)
        own_weights = lax.dynamic_slice_in_dim(weights_flat, row_offset, row_share_count, 0)
        own_scaled = (own_weights[:, None] * own_sum).astype(jnp.bfloat16)
        scaled = gather_directly(own_scaled, COL, 0).reshape(row_blocks, block_width, directions)
        picked_rows = scaled[block_row]
        backward = jnp.einsum(
            "bji,bjk->bik", x_blocks, picked_rows, preferred_element_type=jnp.float32
        )
        summed = jnp.einsum("bc,bik->cik", column_select, backward, precision=highest)
        hessian_image = (
            sent_and_summed(summed.reshape(feature_rows, directions), ROW, 0)
            + ridge_weight * direction
        )
        own_residual = residual
        curvature, cross_term, image_square = (
            by_axis(jnp.sum(direction * hessian_image, axis=0), ROW_COL),
            by_axis(jnp.sum(own_residual * hessian_image, axis=0), ROW_COL),
            by_axis(jnp.sum(hessian_image * hessian_image, axis=0), ROW_COL),
        )
        step_size = norm_now / curvature
        norm_next = norm_now - 2.0 * step_size * cross_term + step_size * step_size * image_square
        solution = solution + step_size * direction
        residual = residual - step_size * hessian_image
        if iteration + 1 < ITERS:
            direction = residual + norm_next / norm_now * direction
            norm_now = norm_next
    solution, residual = tuple(
        (
            part.astype(jnp.float32)
            for part in in_one_piece(
                (solution.astype(jnp.bfloat16), residual.astype(jnp.bfloat16)), ROW, 0, 1
            )
        )
    )
    return (solution, residual)


def solution(mesh):
    torus = Mesh(mesh.devices.reshape(2, 4, 4, 2, 2), ("row_0", "row_1", "col_0", "col_1", "col_2"))
    in_specs = (P(ROW, COL, None), P(ROW, COL), P(ROW), P(ROW), P(COL, None))
    out_specs = (P(COL, None), P(COL, None))
    return jax.shard_map(
        on_device, mesh=torus, in_specs=in_specs, out_specs=out_specs, check_vma=False
    )
```

profile of v0, /device:TPU:0, one launch (start us, length us, event | category | flops | bytes accessed | tf_op | source)
XLA Modules:
  0.0 715.4 jit_solution(13770284594476689411)
XLA Ops:
  9.0 6.4 all-to-all-start
  16.1 8.9 %all-to-all-done = bf16[8,256,128]{2,1,0:T(8,128)(2,1)S(1)} async-done(((bf16[8,256,128]{2,1,0:T(8,128)(2,1)}), bf16[8,256,128]{2,1,0:T(8,128)(2,1)S(1)}, u32[]{:S(2)}, u32[]{:S(2)}) %all-to-all-start) | async-done | bytes 524320 | tf_op jit(solution)/shard_map/all_to_all | solution.py:28
  24.9 8.6 %gather_fusion = bf16[256,128,128]{2,1,0:T(8,128)(2,1)} fusion(bf16[16,128,128]{2,1,0:T(8,128)(2,1)S(1)} %bitcast.56, s32[1024]{0:T(1024)S(1)} %pad_clamp_fusion.1), kind=kCustom, calls=%fused_computation | custom fusion | bytes 16778240 | tf_op jit(solution)/shard_map/gather | solution.py:91
  33.5 12.8 %convolution_bitcast_fusion.5 = f32[256,128,128]{1,2,0:T(8,128)} fusion(bf16[256,128,128]{2,1,0:T(8,128)(2,1)} %gather_fusion, bf16[256,128,128]{2,1,0:T(8,128)(2,1)} %param.5), kind=kOutput, calls=%fused_computation.11 | convolution fusion | flops 1073741824 | bytes 33554432 | tf_op jit(solution)/shard_map/bij,bjk->bik/dot_general | solution.py:92
  46.4 17.5 %copy.26 = f32[256,128,128]{2,0,1:T(8,128)} copy(f32[256,128,128]{1,2,0:T(8,128)} %convolution_bitcast_fusion.5) | data formatting | bytes 33554432 | tf_op jit(solution)/shard_map/bij,bjk->bik/dot_general | solution.py:92
  63.8 9.8 %fusion.5 = f32[32,128,128]{2,0,1:T(8,128)S(1)} fusion(f32[256,128,128]{2,0,1:T(8,128)} %copy.26, s32[256]{0:T(256)S(1)} %bitcast.71), kind=kOutput, calls=%fused_computation.40 | convolution fusion | flops 1610620928 | bytes 18875392 | tf_op jit(solution)/shard_map/br,bik->rik/dot_general | solution.py:95
  73.6 2.6 copy.27
  76.2 6.7 all-to-all-start.1
  83.0 1.5 compare_reduce_fusion
  84.6 27.5 %all-to-all-done.1 = f32[16,256,128]{2,1,0:T(8,128)S(1)} async-done(((f32[16,256,128]{2,1,0:T(8,128)}), f32[16,256,128]{2,1,0:T(8,128)S(1)}, u32[]{:S(2)}, u32[]{:S(2)}) %all-to-all-start.1) | async-done | bytes 2097184 | tf_op jit(solution)/shard_map/all_to_all | solution.py:22
  112.4 1.2 broadcast_in_dim.18
  113.5 4.9 all-to-all-start.2
  118.7 17.7 %all-to-all-done.2 = bf16[16,256,128]{2,1,0:T(8,128)(2,1)S(1)} async-done(((bf16[16,256,128]{2,1,0:T(8,128)(2,1)}), bf16[16,256,128]{2,1,0:T(8,128)(2,1)S(1)}, u32[]{:S(2)}, u32[]{:S(2)}) %all-to-all-start.2) | async-done | bytes 1048608 | tf_op jit(solution)/shard_map/all_to_all | solution.py:28
  136.4 8.6 %gather_fusion.1 = bf16[256,128,128]{2,1,0:T(8,128)(2,1)} fusion(bf16[32,128,128]{2,1,0:T(8,128)(2,1)S(1)} %bitcast.59, s32[1024]{0:T(1024)S(1)} %pad_clamp_fusion), kind=kCustom, calls=%fused_computation.1 | custom fusion | bytes 16778240 | tf_op jit(solution)/shard_map/gather | solution.py:101
  145.0 14.4 %convolution_bitcast_fusion.4 = f32[256,128,128]{1,2,0:T(8,128)} fusion(bf16[256,128,128]{2,1,0:T(8,128)(2,1)} %gather_fusion.1, bf16[256,128,128]{2,1,0:T(8,128)(2,1)} %param.5), kind=kOutput, calls=%fused_computation.10 | convolution fusion | flops 1073741824 | bytes 33554432 | tf_op jit(solution)/shard_map/bji,bjk->bik/dot_general | solution.py:102
  159.4 17.5 %copy.29 = f32[256,128,128]{2,0,1:T(8,128)} copy(f32[256,128,128]{1,2,0:T(8,128)} %convolution_bitcast_fusion.4) | data formatting | bytes 33554432 | tf_op jit(solution)/shard_map/bji,bjk->bik/dot_general | solution.py:102
  176.9 9.0 %fusion.15 = f32[16,128,128]{2,0,1:T(8,128)S(1)} fusion(f32[256,128,128]{2,0,1:T(8,128)} %copy.29, s32[256]{0:T(256)S(1)} %bitcast.68), kind=kOutput, calls=%fused_computation.49 | convolution fusion | flops 805310464 | bytes 17826816 | tf_op jit(solution)/shard_map/bc,bik->cik/dot_general | solution.py:105
  186.3 18.3 %all_to_all.60 = f32[8,256,128]{2,1,0:T(8,128)S(1)} all-to-all(f32[8,256,128]{2,1,0:T(8,128)S(1)} %bitcast.65), channel_id=1, replica_groups=mesh['row_0'=2,'row_1'=4,'col_0'=4,'col_1'=2,'col_2'=2] {'row_0','row_1'}, dimensions={0} | all-to-all | bytes 2097152 | tf_op jit(solution)/shard_map/all_to_all | solution.py:22
  204.6 1.0 multiply_reduce_fusion.4
  205.6 4.9 all-reduce.9
  210.5 8.5 %all-reduce.3 = (f32[128]{0:T(128)S(1)}, f32[128]{0:T(128)S(1)}, f32[128]{0:T(128)S(1)}) all-reduce(f32[128]{0:T(128)S(1)} %get-tuple-element.35, f32[128]{0:T(128)S(1)} %get-tuple-element.36, f32[128]{0:T(128)S(1)} %get-tuple-element.37), channel_id=1, replica_groups=mesh['row_0'=2,'row_1'=4,'col_0'=4,'col_1'=2,'col_2'=2] {'row_1'}, use_global_device_ids=true, to_apply=%region_2.3 | all-reduce | flops 384 | bytes 3072 | tf_op jit(solution)/shard_map/psum | solution.py:46
  219.0 8.7 %all-reduce.1 = (f32[128]{0:T(128)S(1)}, f32[128]{0:T(128)S(1)}, f32[128]{0:T(128)S(1)}) all-reduce(f32[128]{0:T(128)S(1)} %get-tuple-element.17, f32[128]{0:T(128)S(1)} %get-tuple-element.18, f32[128]{0:T(128)S(1)} %get-tuple-element.19), channel_id=1, replica_groups=mesh['row_0'=2,'row_1'=4,'col_0'=4,'col_1'=2,'col_2'=2] {'col_0'}, use_global_device_ids=true, to_apply=%region_3.4 | all-reduce | flops 384 | bytes 3072 | tf_op jit(solution)/shard_map/psum | solution.py:46
  227.7 6.4 all-reduce.7
  234.1 2.4 all-reduce.5
  236.6 0.9 fusion.24
  237.6 13.4 %all_to_all.61 = bf16[8,256,128]{2,1,0:T(8,128)(2,1)S(1)} all-to-all(bf16[8,256,128]{2,1,0:T(8,128)(2,1)S(1)} %broadcast_in_dim.19), channel_id=1, replica_groups=mesh['row_0'=2,'row_1'=4,'col_0'=4,'col_1'=2,'col_2'=2] {'row_0','row_1'}, dimensions={0} | all-to-all | bytes 1048576 | tf_op jit(solution)/shard_map/all_to_all | solution.py:28
  251.0 8.6 %gather_fusion.2 = bf16[256,128,128]{2,1,0:T(8,128)(2,1)} fusion(bf16[16,128,128]{2,1,0:T(8,128)(2,1)S(1)} %bitcast.58, s32[1024]{0:T(1024)S(1)} %pad_clamp_fusion.1), kind=kCustom, calls=%fused_computation.2 | custom fusion | bytes 16778240 | tf_op jit(solution)/shard_map/gather | solution.py:91
  259.6 12.8 %convolution_bitcast_fusion.3 = f32[256,128,128]{1,2,0:T(8,128)} fusion(bf16[256,128,128]{2,1,0:T(8,128)(2,1)} %gather_fusion.2, bf16[256,128,128]{2,1,0:T(8,128)(2,1)} %param.5), kind=kOutput, calls=%fused_computation.9 | convolution fusion | flops 1073741824 | bytes 33554432 | tf_op jit(solution)/shard_map/bij,bjk->bik/dot_general | solution.py:92
  272.4 17.5 %copy.32 = f32[256,128,128]{2,0,1:T(8,128)} copy(f32[256,128,128]{1,2,0:T(8,128)} %convolution_bitcast_fusion.3) | data formatting | bytes 33554432 | tf_op jit(solution)/shard_map/bij,bjk->bik/dot_general | solution.py:92
  289.9 9.8 %fusion.3 = f32[32,128,128]{2,0,1:T(8,128)S(1)} fusion(f32[256,128,128]{2,0,1:T(8,128)} %copy.32, s32[256]{0:T(256)S(1)} %bitcast.72), kind=kOutput, calls=%fused_computation.39 | convolution fusion | flops 1610620928 | bytes 18875392 | tf_op jit(solution)/shard_map/br,bik->rik/dot_general | solution.py:95
  299.7 1.2 copy.33
  300.9 32.3 %all_to_all.62 = f32[16,256,128]{2,1,0:T(8,128)S(1)} all-to-all(f32[16,256,128]{2,1,0:T(8,128)S(1)} %bitcast.63), channel_id=1, replica_groups=mesh['row_0'=2,'row_1'=4,'col_0'=4,'col_1'=2,'col_2'=2] {'col_0','col_1'..., dimensions={0} | all-to-all | bytes 4194304 | tf_op jit(solution)/shard_map/all_to_all | solution.py:22
  333.6 20.8 %all_to_all.63 = bf16[16,256,128]{2,1,0:T(8,128)(2,1)S(1)} all-to-all(bf16[16,256,128]{2,1,0:T(8,128)(2,1)S(1)} %broadcast_in_dim.20), channel_id=1, replica_groups=mesh['row_0'=2,'row_1'=4,'col_0'=4,'col_1'=2,'col_2'=2] {'col_0','col_1'..., dimensions={0} | all-to-all | bytes 2097152 | tf_op jit(solution)/shard_map/all_to_all | solution.py:28
  354.4 8.6 %gather_fusion.3 = bf16[256,128,128]{2,1,0:T(8,128)(2,1)} fusion(bf16[32,128,128]{2,1,0:T(8,128)(2,1)S(1)} %bitcast.61, s32[1024]{0:T(1024)S(1)} %pad_clamp_fusion), kind=kCustom, calls=%fused_computation.3 | custom fusion | bytes 16778240 | tf_op jit(solution)/shard_map/gather | solution.py:101
  363.0 14.4 %convolution_bitcast_fusion.2 = f32[256,128,128]{1,2,0:T(8,128)} fusion(bf16[256,128,128]{2,1,0:T(8,128)(2,1)} %gather_fusion.3, bf16[256,128,128]{2,1,0:T(8,128)(2,1)} %param.5), kind=kOutput, calls=%fused_computation.8 | convolution fusion | flops 1073741824 | bytes 33554432 | tf_op jit(solution)/shard_map/bji,bjk->bik/dot_general | solution.py:102
  377.4 17.5 %copy.35 = f32[256,128,128]{2,0,1:T(8,128)} copy(f32[256,128,128]{1,2,0:T(8,128)} %convolution_bitcast_fusion.2) | data formatting | bytes 33554432 | tf_op jit(solution)/shard_map/bji,bjk->bik/dot_general | solution.py:102
  394.8 9.0 %fusion.13 = f32[16,128,128]{2,0,1:T(8,128)S(1)} fusion(f32[256,128,128]{2,0,1:T(8,128)} %copy.35, s32[256]{0:T(256)S(1)} %bitcast.69), kind=kOutput, calls=%fused_computation.48 | convolution fusion | flops 805310464 | bytes 17826816 | tf_op jit(solution)/shard_map/bc,bik->cik/dot_general | solution.py:105
  404.2 17.7 %all_to_all.64 = f32[8,256,128]{2,1,0:T(8,128)S(1)} all-to-all(f32[8,256,128]{2,1,0:T(8,128)S(1)} %bitcast.66), channel_id=1, replica_groups=mesh['row_0'=2,'row_1'=4,'col_0'=4,'col_1'=2,'col_2'=2] {'row_0','row_1'}, dimensions={0} | all-to-all | bytes 2097152 | tf_op jit(solution)/shard_map/all_to_all | solution.py:22
  422.0 4.9 all-reduce.8
  427.0 8.5 %all-reduce.2 = (f32[128]{0:T(128)S(1)}, f32[128]{0:T(128)S(1)}, f32[128]{0:T(128)S(1)}) all-reduce(f32[128]{0:T(128)S(1)} %get-tuple-element.32, f32[128]{0:T(128)S(1)} %get-tuple-element.33, f32[128]{0:T(128)S(1)} %get-tuple-element.34), channel_id=1, replica_groups=mesh['row_0'=2,'row_1'=4,'col_0'=4,'col_1'=2,'col_2'=2] {'row_1'}, use_global_device_ids=true, to_apply=%region_37.38 | all-reduce | flops 384 | bytes 3072 | tf_op jit(solution)/shard_map/psum | solution.py:46
  435.5 8.8 %all-reduce = (f32[128]{0:T(128)S(1)}, f32[128]{0:T(128)S(1)}, f32[128]{0:T(128)S(1)}) all-reduce(f32[128]{0:T(128)S(1)} %get-tuple-element.14, f32[128]{0:T(128)S(1)} %get-tuple-element.15, f32[128]{0:T(128)S(1)} %get-tuple-element.16), channel_id=1, replica_groups=mesh['row_0'=2,'row_1'=4,'col_0'=4,'col_1'=2,'col_2'=2] {'col_0'}, use_global_device_ids=true, to_apply=%region_38.39 | all-reduce | flops 384 | bytes 3072 | tf_op jit(solution)/shard_map/psum | solution.py:46
  444.3 6.4 all-reduce.6
  450.7 2.4 all-reduce.4
  453.3 13.2 %all_to_all.65 = bf16[8,256,128]{2,1,0:T(8,128)(2,1)S(1)} all-to-all(bf16[8,256,128]{2,1,0:T(8,128)(2,1)S(1)} %broadcast_in_dim.21), channel_id=1, replica_groups=mesh['row_0'=2,'row_1'=4,'col_0'=4,'col_1'=2,'col_2'=2] {'row_0','row_1'}, dimensions={0} | all-to-all | bytes 1048576 | tf_op jit(solution)/shard_map/all_to_all | solution.py:28
  466.5 8.6 %gather_fusion.4 = bf16[256,128,128]{2,1,0:T(8,128)(2,1)} fusion(bf16[16,128,128]{2,1,0:T(8,128)(2,1)S(1)} %bitcast.57, s32[1024]{0:T(1024)S(1)} %pad_clamp_fusion.1), kind=kCustom, calls=%fused_computation.4 | custom fusion | bytes 16778240 | tf_op jit(solution)/shard_map/gather | solution.py:91
  475.1 12.8 %convolution_bitcast_fusion.1 = f32[256,128,128]{1,2,0:T(8,128)} fusion(bf16[256,128,128]{2,1,0:T(8,128)(2,1)} %gather_fusion.4, bf16[256,128,128]{2,1,0:T(8,128)(2,1)} %param.5), kind=kOutput, calls=%fused_computation.7 | convolution fusion | flops 1073741824 | bytes 33554432 | tf_op jit(solution)/shard_map/bij,bjk->bik/dot_general | solution.py:92
  487.9 17.5 %copy.38 = f32[256,128,128]{2,0,1:T(8,128)} copy(f32[256,128,128]{1,2,0:T(8,128)} %convolution_bitcast_fusion.1) | data formatting | bytes 33554432 | tf_op jit(solution)/shard_map/bij,bjk->bik/dot_general | solution.py:92
  505.4 9.7 %fusion.1 = f32[32,128,128]{2,0,1:T(8,128)S(1)} fusion(f32[256,128,128]{2,0,1:T(8,128)} %copy.38, s32[256]{0:T(256)S(1)} %bitcast.73), kind=kOutput, calls=%fused_computation.38 | convolution fusion | flops 1610620928 | bytes 18875392 | tf_op jit(solution)/shard_map/br,bik->rik/dot_general | solution.py:95
  515.2 1.2 copy.39
  516.4 32.4 %all_to_all.66 = f32[16,256,128]{2,1,0:T(8,128)S(1)} all-to-all(f32[16,256,128]{2,1,0:T(8,128)S(1)} %bitcast.64), channel_id=1, replica_groups=mesh['row_0'=2,'row_1'=4,'col_0'=4,'col_1'=2,'col_2'=2] {'col_0','col_1'..., dimensions={0} | all-to-all | bytes 4194304 | tf_op jit(solution)/shard_map/all_to_all | solution.py:22
  549.2 20.8 %all_to_all.67 = bf16[16,256,128]{2,1,0:T(8,128)(2,1)S(1)} all-to-all(bf16[16,256,128]{2,1,0:T(8,128)(2,1)S(1)} %broadcast_in_dim.22), channel_id=1, replica_groups=mesh['row_0'=2,'row_1'=4,'col_0'=4,'col_1'=2,'col_2'=2] {'col_0','col_1'..., dimensions={0} | all-to-all | bytes 2097152 | tf_op jit(solution)/shard_map/all_to_all | solution.py:28
  570.0 8.6 %gather_fusion.5 = bf16[256,128,128]{2,1,0:T(8,128)(2,1)} fusion(bf16[32,128,128]{2,1,0:T(8,128)(2,1)S(1)} %bitcast.60, s32[1024]{0:T(1024)S(1)} %pad_clamp_fusion), kind=kCustom, calls=%fused_computation.5 | custom fusion | bytes 16778240 | tf_op jit(solution)/shard_map/gather | solution.py:101
  578.7 14.4 %convolution_bitcast_fusion = f32[256,128,128]{1,2,0:T(8,128)} fusion(bf16[256,128,128]{2,1,0:T(8,128)(2,1)} %gather_fusion.5, bf16[256,128,128]{2,1,0:T(8,128)(2,1)} %param.5), kind=kOutput, calls=%fused_computation.6 | convolution fusion | flops 1073741824 | bytes 33554432 | tf_op jit(solution)/shard_map/bji,bjk->bik/dot_general | solution.py:102
  593.0 17.5 %copy.41 = f32[256,128,128]{2,0,1:T(8,128)} copy(f32[256,128,128]{1,2,0:T(8,128)} %convolution_bitcast_fusion) | data formatting | bytes 33554432 | tf_op jit(solution)/shard_map/bji,bjk->bik/dot_general | solution.py:102
  610.5 9.0 %fusion.11 = f32[16,128,128]{2,0,1:T(8,128)S(1)} fusion(f32[256,128,128]{2,0,1:T(8,128)} %copy.41, s32[256]{0:T(256)S(1)} %bitcast.70), kind=kOutput, calls=%fused_computation.47 | convolution fusion | flops 805310464 | bytes 17826816 | tf_op jit(solution)/shard_map/bc,bik->cik/dot_general | solution.py:105
  619.9 17.7 %all_to_all.68 = f32[8,256,128]{2,1,0:T(8,128)S(1)} all-to-all(f32[8,256,128]{2,1,0:T(8,128)S(1)} %bitcast.67), channel_id=1, replica_groups=mesh['row_0'=2,'row_1'=4,'col_0'=4,'col_1'=2,'col_2'=2] {'row_0','row_1'}, dimensions={0} | all-to-all | bytes 2097152 | tf_op jit(solution)/shard_map/all_to_all | solution.py:22
  637.7 4.9 psum.290
  642.6 8.5 %psum.291 = f32[128]{0:T(128)S(1)} all-reduce(f32[128]{0:T(128)S(1)} %psum.290), channel_id=1, replica_groups=mesh['row_0'=2,'row_1'=4,'col_0'=4,'col_1'=2,'col_2'=2] {'row_1'}, use_global_device_ids=true, to_apply=%region_45.46 | all-reduce | flops 128 | bytes 1024 | tf_op jit(solution)/shard_map/psum | solution.py:46
  651.1 8.8 %psum.292 = f32[128]{0:T(128)S(1)} all-reduce(f32[128]{0:T(128)S(1)} %psum.291), channel_id=1, replica_groups=mesh['row_0'=2,'row_1'=4,'col_0'=4,'col_1'=2,'col_2'=2] {'col_0'}, use_global_device_ids=true, to_apply=%region_46.47 | all-reduce | flops 128 | bytes 1024 | tf_op jit(solution)/shard_map/psum | solution.py:46
  659.9 6.4 psum.293
  666.3 2.4 psum.294
  668.8 1.0 add_convert_fusion
  670.5 35.0 %all-gather.2.cloned.1.call-done = bf16[2048,256]{1,0:T(8,128)(2,1)} async-done(((bf16[256,256]{1,0:T(8,128)(2,1)}), bf16[2048,256]{1,0:T(8,128)(2,1)}) %all-gather.2.cloned.1.call-update) | async-done | bytes 1048592 | tf_op jit(solution)/shard_map/all_gather | solution.py:52
  705.5 2.7 slice_convert_fusion
  (38 shorter events, 6.0 us)
Async XLA Ops:
  9.0 16.0 %all-to-all-start = ((bf16[8,256,128]{2,1,0:T(8,128)(2,1)}), bf16[8,256,128]{2,1,0:T(8,128)(2,1)S(1)}, u32[]{:S(2)}, u32[]{:S(2)}) async-start(bf16[8,256,128]{2,1,0:T(8,128)(2,1)} %broadcast_in_dim.17), calls=%async_computation | async-start | bytes 1048576 | tf_op jit(solution)/shard_map/all_to_all | solution.py:28
  73.6 9.3 %copy-start = (f32[4096]{0:T(1024)S(1)}, f32[4096]{0:T(1024)}, u32[]{:S(2)}) copy-start(f32[4096]{0:T(1024)} %param.7) | copy-start | bytes 49156
  73.6 9.3 %copy-start.1 = (s32[512]{0:T(512)S(1)}, s32[512]{0:T(512)}, u32[]{:S(2)}) copy-start(s32[512]{0:T(512)} %param.8) | copy-start | bytes 6148
  76.2 36.0 %all-to-all-start.1 = ((f32[16,256,128]{2,1,0:T(8,128)}), f32[16,256,128]{2,1,0:T(8,128)S(1)}, u32[]{:S(2)}, u32[]{:S(2)}) async-start(f32[16,256,128]{2,1,0:T(8,128)} %bitcast.62), calls=%async_computation.1 | async-start | bytes 4194304 | tf_op jit(solution)/shard_map/all_to_all | solution.py:22
  113.5 22.9 %all-to-all-start.2 = ((bf16[16,256,128]{2,1,0:T(8,128)(2,1)}), bf16[16,256,128]{2,1,0:T(8,128)(2,1)S(1)}, u32[]{:S(2)}, u32[]{:S(2)}) async-start(bf16[16,256,128]{2,1,0:T(8,128)(2,1)} %broadcast_in_dim.18), calls=%async_computation.2 | async-start | bytes 2097152 | tf_op jit(solution)/shard_map/all_to_all | solution.py:28
  118.4 587.1 %all-gather.2.cloned.1.call-start = ((), (), s32[]{:S(2)}) async-start(), calls=%async_computation.12 | async-start | bytes 1179648 | tf_op jit(solution)/shard_map/all_gather | solution.py:52
Sparse Core Ops, SparseCore 0:
  670.6 34.8 all-gather.1
where the time goes:
time: 726 us; the launch traced here: 715 us
  blocking collectives  280 us (39%)
  local copies, waits for them, and re-layouts  166 us (23%)
  matrix products  138 us (19%)
  waiting for transfers between devices  89.2 us (12%)
  starting transfers between devices  18.2 us (3%)
  between operations  14.7 us (2%)
  other arithmetic  9.51 us (1%)
    all_to_all x5, blocking collectives, sent_and_summed(): lax.all_to_all(pieces, axis, split_axis=0, concat_axis=0, tiled=True)  118 us
    psum x15, blocking collectives, by_axis(): shard = lax.psum(shard, axis)  93.2 us
    all_to_all x4, blocking collectives, from_everyone(): lax.all_to_all(jnp.broadcast_to(shard[None], (size, *shard.shape)), axis,...  68.2 us
    dot_general x3, local copies, waits for them, and re-layouts, on_device(): jnp.einsum('bij,bjk->bik', x_blocks, picked_tiles, preferred_element_type...  52.4 us
    dot_general x3, local copies, waits for them, and re-layouts, on_device(): jnp.einsum('bji,bjk->bik', x_blocks, picked_rows, preferred_element_type=...  52.4 us
    dot_general x3, matrix products, on_device(): jnp.einsum('bji,bjk->bik', x_blocks, picked_rows, preferred_element_type=...  43.1 us
    dot_general x3, matrix products, on_device(): jnp.einsum('bij,bjk->bik', x_blocks, picked_tiles, preferred_element_type...  38.5 us
    all_gather x1, waiting for transfers between devices, in_one_piece(): result, at, outs = (lax.all_gather(both, axis, axis=dim, tiled=True), 0, [])  35 us
  transfers between devices with their start and end apart: 4, of which 4 were waited for; matrix products, arithmetic and copies ran while one was open for 0% of the time, Pallas kernels for 0%

commit v1 on v0

--- a/solution.py
+++ b/solution.py
@@ -43,7 +43,7 @@
 
 def by_axis(shard, axes):
     for axis in axes:
-        shard = lax.psum(shard, axis)
+        shard = lax.all_gather(shard, axis).sum(axis=0)
     return shard
 
 

time: 726 us -> 826 us (1.14)
  blocking collectives: 280 us -> 379 us
    all_gather x0 -> x35, blocking collectives: none -> 192 us  [by_axis(): shard = lax.all_gather(shard, axis).sum(axis=0)]
    psum x15 -> x0, blocking collectives: 93.2 us -> none  [by_axis(): shard = lax.psum(shard, axis)]
where the time goes in v1:
time: 826 us; the launch traced here: 815 us
  blocking collectives  379 us (46%)
  local copies, waits for them, and re-layouts  166 us (20%)
  matrix products  138 us (17%)
  waiting for transfers between devices  89.2 us (11%)
  starting transfers between devices  18.2 us (2%)
  between operations  14.8 us (2%)
  other arithmetic  10.2 us (1%)
    all_gather x35, blocking collectives, by_axis(): shard = lax.all_gather(shard, axis).sum(axis=0)  192 us
    all_to_all x5, blocking collectives, sent_and_summed(): lax.all_to_all(pieces, axis, split_axis=0, concat_axis=0, tiled=True)  118 us
    all_to_all x4, blocking collectives, from_everyone(): lax.all_to_all(jnp.broadcast_to(shard[None], (size, *shard.shape)), axis,...  68.3 us
    dot_general x3, local copies, waits for them, and re-layouts, on_device(): jnp.einsum('bij,bjk->bik', x_blocks, picked_tiles, preferred_element_type...  52.4 us
    dot_general x3, local copies, waits for them, and re-layouts, on_device(): jnp.einsum('bji,bjk->bik', x_blocks, picked_rows, preferred_element_type=...  52.4 us
    dot_general x3, matrix products, on_device(): jnp.einsum('bji,bjk->bik', x_blocks, picked_rows, preferred_element_type=...  43.1 us
    dot_general x3, matrix products, on_device(): jnp.einsum('bij,bjk->bik', x_blocks, picked_tiles, preferred_element_type...  38.5 us
    all_gather x1, waiting for transfers between devices, in_one_piece(): result, at, outs = (lax.all_gather(both, axis, axis=dim, tiled=True), 0, [])  35 us
  transfers between devices with their start and end apart: 4, of which 4 were waited for; matrix products, arithmetic and copies ran while one was open for 0% of the time, Pallas kernels for 0%

profile of v1, /device:TPU:0, one launch (start us, length us, event | category | flops | bytes accessed | tf_op | source)
XLA Modules:
  0.0 815.1 jit_solution(14818144485708421496)
XLA Ops:
  9.0 6.4 all-to-all-start
  16.1 8.9 %all-to-all-done = bf16[8,256,128]{2,1,0:T(8,128)(2,1)S(1)} async-done(((bf16[8,256,128]{2,1,0:T(8,128)(2,1)}), bf16[8,256,128]{2,1,0:T(8,128)(2,1)S(1)}, u32[]{:S(2)}, u32[]{:S(2)}) %all-to-all-start) | async-done | bytes 524320 | tf_op jit(solution)/shard_map/all_to_all | solution.py:28
  24.9 8.6 %gather_fusion = bf16[256,128,128]{2,1,0:T(8,128)(2,1)} fusion(bf16[16,128,128]{2,1,0:T(8,128)(2,1)S(1)} %bitcast.91, s32[1024]{0:T(1024)S(1)} %pad_clamp_fusion.1), kind=kCustom, calls=%fused_computation | custom fusion | bytes 16778240 | tf_op jit(solution)/shard_map/gather | solution.py:91
  33.5 12.8 %convolution_bitcast_fusion.5 = f32[256,128,128]{1,2,0:T(8,128)} fusion(bf16[256,128,128]{2,1,0:T(8,128)(2,1)} %gather_fusion, bf16[256,128,128]{2,1,0:T(8,128)(2,1)} %param.5), kind=kOutput, calls=%fused_computation.11 | convolution fusion | flops 1073741824 | bytes 33554432 | tf_op jit(solution)/shard_map/bij,bjk->bik/dot_general | solution.py:92
  46.4 17.5 %copy.44 = f32[256,128,128]{2,0,1:T(8,128)} copy(f32[256,128,128]{1,2,0:T(8,128)} %convolution_bitcast_fusion.5) | data formatting | bytes 33554432 | tf_op jit(solution)/shard_map/bij,bjk->bik/dot_general | solution.py:92
  63.8 9.8 %fusion.5 = f32[32,128,128]{2,0,1:T(8,128)S(1)} fusion(f32[256,128,128]{2,0,1:T(8,128)} %copy.44, s32[256]{0:T(256)S(1)} %bitcast.106), kind=kOutput, calls=%fused_computation.40 | convolution fusion | flops 1610620928 | bytes 18875392 | tf_op jit(solution)/shard_map/br,bik->rik/dot_general | solution.py:95
  76.2 6.7 all-to-all-start.1
  84.6 27.5 %all-to-all-done.1 = f32[16,256,128]{2,1,0:T(8,128)S(1)} async-done(((f32[16,256,128]{2,1,0:T(8,128)}), f32[16,256,128]{2,1,0:T(8,128)S(1)}, u32[]{:S(2)}, u32[]{:S(2)}) %all-to-all-start.1) | async-done | bytes 2097184 | tf_op jit(solution)/shard_map/all_to_all | solution.py:22
  113.5 4.9 all-to-all-start.2
  118.7 17.7 %all-to-all-done.2 = bf16[16,256,128]{2,1,0:T(8,128)(2,1)S(1)} async-done(((bf16[16,256,128]{2,1,0:T(8,128)(2,1)}), bf16[16,256,128]{2,1,0:T(8,128)(2,1)S(1)}, u32[]{:S(2)}, u32[]{:S(2)}) %all-to-all-start.2) | async-done | bytes 1048608 | tf_op jit(solution)/shard_map/all_to_all | solution.py:28
  136.4 8.6 %gather_fusion.1 = bf16[256,128,128]{2,1,0:T(8,128)(2,1)} fusion(bf16[32,128,128]{2,1,0:T(8,128)(2,1)S(1)} %bitcast.94, s32[1024]{0:T(1024)S(1)} %pad_clamp_fusion), kind=kCustom, calls=%fused_computation.1 | custom fusion | bytes 16778240 | tf_op jit(solution)/shard_map/gather | solution.py:101
  145.0 14.4 %convolution_bitcast_fusion.4 = f32[256,128,128]{1,2,0:T(8,128)} fusion(bf16[256,128,128]{2,1,0:T(8,128)(2,1)} %gather_fusion.1, bf16[256,128,128]{2,1,0:T(8,128)(2,1)} %param.5), kind=kOutput, calls=%fused_computation.10 | convolution fusion | flops 1073741824 | bytes 33554432 | tf_op jit(solution)/shard_map/bji,bjk->bik/dot_general | solution.py:102
  159.4 17.5 %copy.47 = f32[256,128,128]{2,0,1:T(8,128)} copy(f32[256,128,128]{1,2,0:T(8,128)} %convolution_bitcast_fusion.4) | data formatting | bytes 33554432 | tf_op jit(solution)/shard_map/bji,bjk->bik/dot_general | solution.py:102
  176.9 9.0 %fusion.15 = f32[16,128,128]{2,0,1:T(8,128)S(1)} fusion(f32[256,128,128]{2,0,1:T(8,128)} %copy.47, s32[256]{0:T(256)S(1)} %bitcast.103), kind=kOutput, calls=%fused_computation.49 | convolution fusion | flops 805310464 | bytes 17826816 | tf_op jit(solution)/shard_map/bc,bik->cik/dot_general | solution.py:105
  186.3 18.3 %all_to_all.60 = f32[8,256,128]{2,1,0:T(8,128)S(1)} all-to-all(f32[8,256,128]{2,1,0:T(8,128)S(1)} %bitcast.100), channel_id=1, replica_groups=mesh['row_0'=2,'row_1'=4,'col_0'=4,'col_1'=2,'col_2'=2] {'row_0','row_1'}, dimensions={0} | all-to-all | bytes 2097152 | tf_op jit(solution)/shard_map/all_to_all | solution.py:22
  205.6 4.2 all-gather.40
  209.8 4.2 all-gather.45
  218.3 7.7 all-gather.36
  226.0 7.8 all-gather.37
  233.9 5.7 all-gather.38
  241.4 8.1 all-gather.46
  249.5 8.0 all-gather.47
  257.5 5.7 all-gather.48
  265.1 7.7 all-gather.41
  272.8 7.8 all-gather.42
  280.7 5.7 all-gather.43
  289.2 13.4 %all_to_all.61 = bf16[8,256,128]{2,1,0:T(8,128)(2,1)S(1)} all-to-all(bf16[8,256,128]{2,1,0:T(8,128)(2,1)S(1)} %broadcast_in_dim.19), channel_id=1, replica_groups=mesh['row_0'=2,'row_1'=4,'col_0'=4,'col_1'=2,'col_2'=2] {'row_0','row_1'}, dimensions={0} | all-to-all | bytes 1048576 | tf_op jit(solution)/shard_map/all_to_all | solution.py:28
  302.6 8.6 %gather_fusion.2 = bf16[256,128,128]{2,1,0:T(8,128)(2,1)} fusion(bf16[16,128,128]{2,1,0:T(8,128)(2,1)S(1)} %bitcast.93, s32[1024]{0:T(1024)S(1)} %pad_clamp_fusion.1), kind=kCustom, calls=%fused_computation.2 | custom fusion | bytes 16778240 | tf_op jit(solution)/shard_map/gather | solution.py:91
  311.2 12.8 %convolution_bitcast_fusion.3 = f32[256,128,128]{1,2,0:T(8,128)} fusion(bf16[256,128,128]{2,1,0:T(8,128)(2,1)} %gather_fusion.2, bf16[256,128,128]{2,1,0:T(8,128)(2,1)} %param.5), kind=kOutput, calls=%fused_computation.9 | convolution fusion | flops 1073741824 | bytes 33554432 | tf_op jit(solution)/shard_map/bij,bjk->bik/dot_general | solution.py:92
  324.0 17.5 %copy.50 = f32[256,128,128]{2,0,1:T(8,128)} copy(f32[256,128,128]{1,2,0:T(8,128)} %convolution_bitcast_fusion.3) | data formatting | bytes 33554432 | tf_op jit(solution)/shard_map/bij,bjk->bik/dot_general | solution.py:92
  341.5 9.8 %fusion.3 = f32[32,128,128]{2,0,1:T(8,128)S(1)} fusion(f32[256,128,128]{2,0,1:T(8,128)} %copy.50, s32[256]{0:T(256)S(1)} %bitcast.107), kind=kOutput, calls=%fused_computation.39 | convolution fusion | flops 1610620928 | bytes 18875392 | tf_op jit(solution)/shard_map/br,bik->rik/dot_general | solution.py:95
  352.5 32.3 %all_to_all.62 = f32[16,256,128]{2,1,0:T(8,128)S(1)} all-to-all(f32[16,256,128]{2,1,0:T(8,128)S(1)} %bitcast.98), channel_id=1, replica_groups=mesh['row_0'=2,'row_1'=4,'col_0'=4,'col_1'=2,'col_2'=2] {'col_0','col_1'..., dimensions={0} | all-to-all | bytes 4194304 | tf_op jit(solution)/shard_map/all_to_all | solution.py:22
  385.2 20.8 %all_to_all.63 = bf16[16,256,128]{2,1,0:T(8,128)(2,1)S(1)} all-to-all(bf16[16,256,128]{2,1,0:T(8,128)(2,1)S(1)} %broadcast_in_dim.20), channel_id=1, replica_groups=mesh['row_0'=2,'row_1'=4,'col_0'=4,'col_1'=2,'col_2'=2] {'col_0','col_1'..., dimensions={0} | all-to-all | bytes 2097152 | tf_op jit(solution)/shard_map/all_to_all | solution.py:28
  406.0 8.6 %gather_fusion.3 = bf16[256,128,128]{2,1,0:T(8,128)(2,1)} fusion(bf16[32,128,128]{2,1,0:T(8,128)(2,1)S(1)} %bitcast.96, s32[1024]{0:T(1024)S(1)} %pad_clamp_fusion), kind=kCustom, calls=%fused_computation.3 | custom fusion | bytes 16778240 | tf_op jit(solution)/shard_map/gather | solution.py:101
  414.6 14.4 %convolution_bitcast_fusion.2 = f32[256,128,128]{1,2,0:T(8,128)} fusion(bf16[256,128,128]{2,1,0:T(8,128)(2,1)} %gather_fusion.3, bf16[256,128,128]{2,1,0:T(8,128)(2,1)} %param.5), kind=kOutput, calls=%fused_computation.8 | convolution fusion | flops 1073741824 | bytes 33554432 | tf_op jit(solution)/shard_map/bji,bjk->bik/dot_general | solution.py:102
  429.0 17.5 %copy.53 = f32[256,128,128]{2,0,1:T(8,128)} copy(f32[256,128,128]{1,2,0:T(8,128)} %convolution_bitcast_fusion.2) | data formatting | bytes 33554432 | tf_op jit(solution)/shard_map/bji,bjk->bik/dot_general | solution.py:102
  446.5 9.0 %fusion.13 = f32[16,128,128]{2,0,1:T(8,128)S(1)} fusion(f32[256,128,128]{2,0,1:T(8,128)} %copy.53, s32[256]{0:T(256)S(1)} %bitcast.104), kind=kOutput, calls=%fused_computation.48 | convolution fusion | flops 805310464 | bytes 17826816 | tf_op jit(solution)/shard_map/bc,bik->cik/dot_general | solution.py:105
  455.9 17.7 %all_to_all.64 = f32[8,256,128]{2,1,0:T(8,128)S(1)} all-to-all(f32[8,256,128]{2,1,0:T(8,128)S(1)} %bitcast.101), channel_id=1, replica_groups=mesh['row_0'=2,'row_1'=4,'col_0'=4,'col_1'=2,'col_2'=2] {'row_0','row_1'}, dimensions={0} | all-to-all | bytes 2097152 | tf_op jit(solution)/shard_map/all_to_all | solution.py:22
  473.6 4.2 all-gather.60
  486.3 7.7 all-gather.51
  494.1 8.0 all-gather.52
  502.1 5.7 all-gather.53
  509.6 8.1 all-gather.56
  517.7 7.9 all-gather.57
  525.6 5.7 all-gather.58
  533.1 7.7 all-gather.61
  540.9 8.0 all-gather.62
  548.9 5.7 all-gather.63
  556.5 13.3 %all_to_all.65 = bf16[8,256,128]{2,1,0:T(8,128)(2,1)S(1)} all-to-all(bf16[8,256,128]{2,1,0:T(8,128)(2,1)S(1)} %broadcast_in_dim.21), channel_id=1, replica_groups=mesh['row_0'=2,'row_1'=4,'col_0'=4,'col_1'=2,'col_2'=2] {'row_0','row_1'}, dimensions={0} | all-to-all | bytes 1048576 | tf_op jit(solution)/shard_map/all_to_all | solution.py:28
  569.8 8.6 %gather_fusion.4 = bf16[256,128,128]{2,1,0:T(8,128)(2,1)} fusion(bf16[16,128,128]{2,1,0:T(8,128)(2,1)S(1)} %bitcast.92, s32[1024]{0:T(1024)S(1)} %pad_clamp_fusion.1), kind=kCustom, calls=%fused_computation.4 | custom fusion | bytes 16778240 | tf_op jit(solution)/shard_map/gather | solution.py:91
  578.4 12.8 %convolution_bitcast_fusion.1 = f32[256,128,128]{1,2,0:T(8,128)} fusion(bf16[256,128,128]{2,1,0:T(8,128)(2,1)} %gather_fusion.4, bf16[256,128,128]{2,1,0:T(8,128)(2,1)} %param.5), kind=kOutput, calls=%fused_computation.7 | convolution fusion | flops 1073741824 | bytes 33554432 | tf_op jit(solution)/shard_map/bij,bjk->bik/dot_general | solution.py:92
  591.2 17.5 %copy.56 = f32[256,128,128]{2,0,1:T(8,128)} copy(f32[256,128,128]{1,2,0:T(8,128)} %convolution_bitcast_fusion.1) | data formatting | bytes 33554432 | tf_op jit(solution)/shard_map/bij,bjk->bik/dot_general | solution.py:92
  608.7 9.8 %fusion.1 = f32[32,128,128]{2,0,1:T(8,128)S(1)} fusion(f32[256,128,128]{2,0,1:T(8,128)} %copy.56, s32[256]{0:T(256)S(1)} %bitcast.108), kind=kOutput, calls=%fused_computation.38 | convolution fusion | flops 1610620928 | bytes 18875392 | tf_op jit(solution)/shard_map/br,bik->rik/dot_general | solution.py:95
  619.7 32.4 %all_to_all.66 = f32[16,256,128]{2,1,0:T(8,128)S(1)} all-to-all(f32[16,256,128]{2,1,0:T(8,128)S(1)} %bitcast.99), channel_id=1, replica_groups=mesh['row_0'=2,'row_1'=4,'col_0'=4,'col_1'=2,'col_2'=2] {'col_0','col_1'..., dimensions={0} | all-to-all | bytes 4194304 | tf_op jit(solution)/shard_map/all_to_all | solution.py:22
  652.5 20.8 %all_to_all.67 = bf16[16,256,128]{2,1,0:T(8,128)(2,1)S(1)} all-to-all(bf16[16,256,128]{2,1,0:T(8,128)(2,1)S(1)} %broadcast_in_dim.22), channel_id=1, replica_groups=mesh['row_0'=2,'row_1'=4,'col_0'=4,'col_1'=2,'col_2'=2] {'col_0','col_1'..., dimensions={0} | all-to-all | bytes 2097152 | tf_op jit(solution)/shard_map/all_to_all | solution.py:28
  673.3 8.6 %gather_fusion.5 = bf16[256,128,128]{2,1,0:T(8,128)(2,1)} fusion(bf16[32,128,128]{2,1,0:T(8,128)(2,1)S(1)} %bitcast.95, s32[1024]{0:T(1024)S(1)} %pad_clamp_fusion), kind=kCustom, calls=%fused_computation.5 | custom fusion | bytes 16778240 | tf_op jit(solution)/shard_map/gather | solution.py:101
  681.9 14.4 %convolution_bitcast_fusion = f32[256,128,128]{1,2,0:T(8,128)} fusion(bf16[256,128,128]{2,1,0:T(8,128)(2,1)} %gather_fusion.5, bf16[256,128,128]{2,1,0:T(8,128)(2,1)} %param.5), kind=kOutput, calls=%fused_computation.6 | convolution fusion | flops 1073741824 | bytes 33554432 | tf_op jit(solution)/shard_map/bji,bjk->bik/dot_general | solution.py:102
  696.3 17.5 %copy.59 = f32[256,128,128]{2,0,1:T(8,128)} copy(f32[256,128,128]{1,2,0:T(8,128)} %convolution_bitcast_fusion) | data formatting | bytes 33554432 | tf_op jit(solution)/shard_map/bji,bjk->bik/dot_general | solution.py:102
  713.8 9.0 %fusion.11 = f32[16,128,128]{2,0,1:T(8,128)S(1)} fusion(f32[256,128,128]{2,0,1:T(8,128)} %copy.59, s32[256]{0:T(256)S(1)} %bitcast.105), kind=kOutput, calls=%fused_computation.47 | convolution fusion | flops 805310464 | bytes 17826816 | tf_op jit(solution)/shard_map/bc,bik->cik/dot_general | solution.py:105
  723.2 17.7 %all_to_all.68 = f32[8,256,128]{2,1,0:T(8,128)S(1)} all-to-all(f32[8,256,128]{2,1,0:T(8,128)S(1)} %bitcast.102), channel_id=1, replica_groups=mesh['row_0'=2,'row_1'=4,'col_0'=4,'col_1'=2,'col_2'=2] {'row_0','row_1'}, dimensions={0} | all-to-all | bytes 2097152 | tf_op jit(solution)/shard_map/all_to_all | solution.py:22
  745.2 7.7 all-gather.66
  752.9 8.0 all-gather.67
  760.9 5.7 all-gather.68
  770.1 35.0 %all-gather.72.cloned.1.call-done = bf16[2048,256]{1,0:T(8,128)(2,1)} async-done(((bf16[256,256]{1,0:T(8,128)(2,1)}), bf16[2048,256]{1,0:T(8,128)(2,1)}) %all-gather.72.cloned.1.call-update) | async-done | bytes 1048592 | tf_op jit(solution)/shard_map/all_gather | solution.py:52
  (93 shorter events, 49.2 us)
Async XLA Ops:
  9.0 16.0 %all-to-all-start = ((bf16[8,256,128]{2,1,0:T(8,128)(2,1)}), bf16[8,256,128]{2,1,0:T(8,128)(2,1)S(1)}, u32[]{:S(2)}, u32[]{:S(2)}) async-start(bf16[8,256,128]{2,1,0:T(8,128)(2,1)} %broadcast_in_dim.17), calls=%async_computation | async-start | bytes 1048576 | tf_op jit(solution)/shard_map/all_to_all | solution.py:28
  73.6 9.3 %copy-start = (f32[4096]{0:T(1024)S(1)}, f32[4096]{0:T(1024)}, u32[]{:S(2)}) copy-start(f32[4096]{0:T(1024)} %param.7) | copy-start | bytes 49156
  73.6 9.3 %copy-start.1 = (s32[512]{0:T(512)S(1)}, s32[512]{0:T(512)}, u32[]{:S(2)}) copy-start(s32[512]{0:T(512)} %param.8) | copy-start | bytes 6148
  76.2 36.0 %all-to-all-start.1 = ((f32[16,256,128]{2,1,0:T(8,128)}), f32[16,256,128]{2,1,0:T(8,128)S(1)}, u32[]{:S(2)}, u32[]{:S(2)}) async-start(f32[16,256,128]{2,1,0:T(8,128)} %bitcast.97), calls=%async_computation.1 | async-start | bytes 4194304 | tf_op jit(solution)/shard_map/all_to_all | solution.py:22
  113.5 22.9 %all-to-all-start.2 = ((bf16[16,256,128]{2,1,0:T(8,128)(2,1)}), bf16[16,256,128]{2,1,0:T(8,128)(2,1)S(1)}, u32[]{:S(2)}, u32[]{:S(2)}) async-start(bf16[16,256,128]{2,1,0:T(8,128)(2,1)} %broadcast_in_dim.18), calls=%async_computation.2 | async-start | bytes 2097152 | tf_op jit(solution)/shard_map/all_to_all | solution.py:28
  118.4 686.7 %all-gather.72.cloned.1.call-start = ((), (), s32[]{:S(2)}) async-start(), calls=%async_computation.12 | async-start | bytes 1179648 | tf_op jit(solution)/shard_map/all_gather | solution.py:52
Sparse Core Ops, SparseCore 0:
  770.2 34.8 all-gather.71
